TPU v7x, 512 devices: a whole 4x4x16 slice. The times are simulated.
512 devices in a mesh: shot: 2 (over core), tx: 8 (over z_hi, y), ty: 32 (over z_lo, x).
Axes of the slice: x: 4, y: 4, z: 16 (z_hi: 2, z_lo: 8; z = z_hi * 8 + z_lo), core: 2. Of those that a mesh axis runs over, the one named last changes fastest.
Arguments:
- forward_fields: float32 [2, 9, 128, 512, 128], P('shot', None, 'tx', 'ty'), may hold values from -6 to 6
- adjoint_fields: float32 [2, 9, 128, 512, 128], P('shot', None, 'tx', 'ty'), may hold values from -6 to 6
- lame_lambda: float32 [128, 512, 128], P('tx', 'ty'), may hold values from 1 to 4
- shear_modulus: float32 [128, 512, 128], P('tx', 'ty'), may hold values from 0.5 to 2
- density: float32 [128, 512, 128], P('tx', 'ty'), may hold values from 1 to 3
- source_cell: int32 [2], P('shot'), may hold values from 0 to 8388607
- source_amp: float32 [2], P('shot'), may hold values from 4 to 12
- receiver_cell: int32 [2, 256], P('shot'), may hold values from 0 to 8388607
- residual_amp: float32 [2, 256], P('shot'), may hold values from -16 to 16
Outputs:
- forward_next: float32 [2, 9, 128, 512, 128], P('shot', None, 'tx', 'ty')
- adjoint_next: float32 [2, 9, 128, 512, 128], P('shot', None, 'tx', 'ty')
- gradient: float32 [3, 128, 512, 128], P(None, 'tx', 'ty')
Inputs may be any that keep to these rules, and one draw needn't show every extreme that they name: `source_cell`: each value is a flat index x * 512 * 128 + y * 128 + z of a grid cell. `receiver_cell`: each value is a flat index x * 512 * 128 + y * 128 + z of a grid cell; receivers may share cells.
All inputs are finite; a program needn't handle non-finite values.
Results may differ from a plain program's by a relative error of at most 0.0001.
Values sent between devices are 32-bit elements; how exact they have to be, the bound alone decides.
A program may use at most 64 MiB of HBM per device.

v0:
```python
import jax
import jax.numpy as jnp
from jax import lax
from jax.sharding import PartitionSpec as P

near_coef = 9.0 / 8.0
far_coef = -1.0 / 24.0
time_step = 0.15


def extended(value, sides, width):
    for axis, dim in sides:
        peers, length = (lax.axis_size(axis), value.shape[dim])
        up = [(i, (i + 1) % peers) for i in range(peers - 1)]
        down = [(j, i) for i, j in up]
        last = lax.slice_in_dim(value, length - width, length, axis=dim)
        initial = lax.slice_in_dim(value, 0, width, axis=dim)
        before = lax.ppermute(last, axis, up)
        after = lax.ppermute(initial, axis, down)
        value = jnp.concatenate([before, value, after], axis=dim)
    return value


def shifted(padded, margin, rim_width, direction, offset):
    rank_count = padded.ndim
    sliced = padded
    for which in range(3):
        length = padded.shape[rank_count - 3 + which] - 2 * margin[which] + 2 * rim_width[which]
        begin_at = margin[which] - rim_width[which] + (offset if which == direction else 0)
        sliced = lax.slice_in_dim(sliced, begin_at, begin_at + length, axis=rank_count - 3 + which)
    return sliced


def depth_table(depth_cells, upward):
    source_row = lax.broadcasted_iota(jnp.int32, (depth_cells, depth_cells), 0)
    target_col = lax.broadcasted_iota(jnp.int32, (depth_cells, depth_cells), 1)
    gap = source_row - target_col
    if upward:
        table = near_coef * (
            (gap == 1).astype(jnp.float32) - (gap == 0).astype(jnp.float32)
        ) + far_coef * ((gap == 2).astype(jnp.float32) - (gap == -1).astype(jnp.float32))
    else:
        table = near_coef * (
            (gap == 0).astype(jnp.float32) - (gap == -1).astype(jnp.float32)
        ) + far_coef * ((gap == 1).astype(jnp.float32) - (gap == -2).astype(jnp.float32))
    return table


def derive(padded, margin, rim_width, direction, upward):
    if direction == 2:
        core = shifted(padded, margin, rim_width, 2, 0)
        return jnp.einsum(
            "...k,ki->...i",
            core,
            depth_table(core.shape[-1], upward),
            precision=lax.Precision.HIGHEST,
        )
    if upward:
        return near_coef * (
            shifted(padded, margin, rim_width, direction, 1)
            - shifted(padded, margin, rim_width, direction, 0)
        ) + far_coef * (
            shifted(padded, margin, rim_width, direction, 2)
            - shifted(padded, margin, rim_width, direction, -1)
        )
    return near_coef * (
        shifted(padded, margin, rim_width, direction, 0)
        - shifted(padded, margin, rim_width, direction, -1)
    ) + far_coef * (
        shifted(padded, margin, rim_width, direction, 1)
        - shifted(padded, margin, rim_width, direction, -2)
    )


def accelerate(stress_ext, buoyancy, margin, rim_width):
    comps = [stress_ext[..., which, :, :, :] for which in range(6)]
    accel_x = (
        derive(comps[0], margin, rim_width, 0, True)
        + derive(comps[3], margin, rim_width, 1, False)
        + derive(comps[4], margin, rim_width, 2, False)
    )
    accel_y = (
        derive(comps[3], margin, rim_width, 0, False)
        + derive(comps[1], margin, rim_width, 1, True)
        + derive(comps[5], margin, rim_width, 2, False)
    )
    accel_z = (
        derive(comps[4], margin, rim_width, 0, False)
        + derive(comps[5], margin, rim_width, 1, False)
        + derive(comps[2], margin, rim_width, 2, True)
    )
    return jnp.stack([accel_x, accel_y, accel_z], axis=-4) * buoyancy


def strain_rates(velocity_ext, margin):
    flat_rim = (0, 0, 0)
    comps = [velocity_ext[..., which, :, :, :] for which in range(3)]
    return jnp.stack(
        [
            derive(comps[0], margin, flat_rim, 0, False),
            derive(comps[1], margin, flat_rim, 1, False),
            derive(comps[2], margin, flat_rim, 2, False),
            derive(comps[0], margin, flat_rim, 1, True)
            + derive(comps[1], margin, flat_rim, 0, True),
            derive(comps[0], margin, flat_rim, 2, True)
            + derive(comps[2], margin, flat_rim, 0, True),
            derive(comps[1], margin, flat_rim, 2, True)
            + derive(comps[2], margin, flat_rim, 1, True),
        ],
        axis=-4,
    )


def new_stress(stress_now, strain, lame_lambda, shear_modulus):
    trace = strain[..., 0, :, :, :] + strain[..., 1, :, :, :] + strain[..., 2, :, :, :]
    normal = stress_now[..., :3, :, :, :] + time_step * (
        lame_lambda * trace[..., None, :, :, :] + 2.0 * shear_modulus * strain[..., :3, :, :, :]
    )
    shear = stress_now[..., 3:, :, :, :] + time_step * shear_modulus * strain[..., 3:, :, :, :]
    return jnp.concatenate([normal, shear], axis=-4)


def image_terms(strain_fwd, stress_adj, accel_fwd, velocity_adj):
    trace_fwd = (
        strain_fwd[..., 0, :, :, :] + strain_fwd[..., 1, :, :, :] + strain_fwd[..., 2, :, :, :]
    )
    trace_adj = (
        stress_adj[..., 0, :, :, :] + stress_adj[..., 1, :, :, :] + stress_adj[..., 2, :, :, :]
    )
    grad_lambda = -time_step * trace_fwd * trace_adj
    grad_shear = -time_step * jnp.sum(strain_fwd * stress_adj, axis=-4)
    grad_density = -time_step * jnp.sum(accel_fwd * velocity_adj, axis=-4)
    return jnp.stack([grad_lambda, grad_shear, grad_density], axis=-4)


def localize(cell_index, x_start, y_start, tile_x, tile_y, width_y, depth_cells):
    plane_size = width_y * depth_cells
    global_x = cell_index // plane_size
    remainder = cell_index % plane_size
    global_y = remainder // depth_cells
    global_z = remainder % depth_cells
    local_x = global_x - x_start
    local_y = global_y - y_start
    inside = (local_x >= 0) & (local_x < tile_x) & (local_y >= 0) & (local_y < tile_y)
    return jnp.where(
        inside, (local_x * tile_y + local_y) * depth_cells + global_z, tile_x * tile_y * depth_cells
    )


def inject(fields, where_cells, amounts):
    field_count, tile_x, tile_y, depth_cells = fields.shape
    column_count = tile_x * tile_y
    column = where_cells // depth_cells
    depth = where_cells % depth_cells
    column_hot = (column[:, None] == lax.broadcasted_iota(jnp.int32, (1, column_count), 1)).astype(
        jnp.float32
    )
    depth_hot = (depth[:, None] == lax.broadcasted_iota(jnp.int32, (1, depth_cells), 1)).astype(
        jnp.float32
    ) * amounts[:, None]
    added = jnp.dot(
        column_hot.T, depth_hot, precision=lax.Precision.HIGHEST, preferred_element_type=jnp.float32
    )
    added = added.reshape(1, tile_x, tile_y, depth_cells)
    return jnp.concatenate([fields[:3], fields[3:6] + added, fields[6:]], axis=0)


def body(
    forward_fields,
    adjoint_fields,
    lame_lambda,
    shear_modulus,
    density,
    source_cell,
    source_amp,
    receiver_cell,
    residual_amp,
):
    shot_count, field_count, tile_x, tile_y, depth_cells = forward_fields.shape
    width_y = tile_y * lax.axis_size("ty")
    x_start = lax.axis_index("tx") * tile_x
    y_start = lax.axis_index("ty") * tile_y
    source_local = localize(source_cell, x_start, y_start, tile_x, tile_y, width_y, depth_cells)
    receiver_local = localize(receiver_cell, x_start, y_start, tile_x, tile_y, width_y, depth_cells)
    forward = jax.vmap(inject)(forward_fields, source_local[:, None], source_amp[:, None])
    adjoint = jax.vmap(inject)(adjoint_fields, receiver_local, residual_amp)
    wavefields = jnp.concatenate([forward, adjoint], axis=0)
    buoyancy = 1.0 / density
    margin = (2, 2, 0)
    stress_ext = extended(wavefields[:, 3:], (("tx", 2), ("ty", 3)), 2)
    acceleration = accelerate(stress_ext, buoyancy, margin, (0, 0, 0))
    velocity = wavefields[:, :3] + time_step * acceleration
    velocity_ext = extended(velocity, (("tx", 2), ("ty", 3)), 2)
    strain = strain_rates(velocity_ext, margin)
    stress = new_stress(wavefields[:, 3:], strain, lame_lambda, shear_modulus)
    local_terms = jnp.sum(
        image_terms(
            strain[:shot_count],
            stress[shot_count:],
            acceleration[:shot_count],
            velocity[shot_count:],
        ),
        axis=0,
    )
    gradient = lax.psum(local_terms, "shot")
    stepped = jnp.concatenate([velocity, stress], axis=1)
    return (stepped[:shot_count], stepped[shot_count:], gradient)


def solution(mesh):
    return jax.shard_map(
        body,
        mesh=mesh,
        in_specs=(
            P("shot", None, "tx", "ty", None),
            P("shot", None, "tx", "ty", None),
            P("tx", "ty", None),
            P("tx", "ty", None),
            P("tx", "ty", None),
            P("shot"),
            P("shot"),
            P("shot", None),
            P("shot", None),
        ),
        out_specs=(
            P("shot", None, "tx", "ty", None),
            P("shot", None, "tx", "ty", None),
            P(None, "tx", "ty", None),
        ),
        check_vma=False,
    )
```

profile of v0, /device:TPU:1, one launch (start us, length us, event | category | flops | bytes accessed | tf_op | source)
XLA Modules:
  0.0 155.1 jit_solution(6553573474216581453)
XLA Ops:
  8.6 0.7 and_select_fusion
  9.6 1.1 fusion.53
  10.6 1.8 %fusion.168 = (f32[1,3,16,16,128]{4,3,2,1,0:T(8,128)S(1)}, f32[1,3,16,16,128]{4,3,2,1,0:T(8,128)S(1)}, f32[1,3,16,16,128]{4,3,2,1,0:T(8,128)S(1)}, f32[1,3,16,16...) fusion(f32[1,9,16,16,128]{4,3,2,1,0:T(8,128)} %param.9, ...), kind=kLoop, calls=%fused_computation.264 | loop fusion | flops 196608 | bytes 4980736 | tf_op jit(solution)/shard_map/vmap()/slice | solution.py:165
  12.5 4.0 %collective-permute-start = (f32[2,6,2,16,128]{4,3,2,1,0:T(8,128)S(1)}, f32[2,6,2,16,128]{4,3,2,1,0:T(8,128)S(1)}, u32[]{:S(2)}, u32[]{:S(2)}) collective-permute-start(f32[2,6,2,16,128]{4,3,2,1,0:T(8,128)S(1)} %get-tuple-element.25), channel_id=1, source_target_pairs={{0,32},{32,64},{64,96},{96,128},{128,160},{160,192},{192,224},{1,3... | collective-permute-start | bytes 589832 | tf_op jit(solution)/shard_map/ppermute | solution.py:18
  16.5 1.3 collective-permute-start.1
  18.1 1.0 collective-permute-done
  19.1 3.8 %collective-permute-done.1 = f32[2,6,2,16,128]{4,3,2,1,0:T(8,128)S(1)} collective-permute-done((f32[2,6,2,16,128]{4,3,2,1,0:T(8,128)S(1)}, f32[2,6,2,16,128]{4,3,2,1,0:T(8,128)S(1)}, u32[]{:S(2)}, u32[]{:S(2)}) %collective-permute-start.1) | collective-permute-done | bytes 196640 | tf_op jit(solution)/shard_map/ppermute | solution.py:19
  23.1 4.1 %collective-permute-start.2 = (f32[2,6,20,2,128]{4,3,2,1,0:T(2,128)S(1)}, f32[2,6,20,2,128]{4,3,2,1,0:T(2,128)S(1)}, u32[]{:S(2)}, u32[]{:S(2)}) collective-permute-start(f32[2,6,20,2,128]{4,3,2,1,0:T(2,128)S(1)} %get-tuple-element.27), channel_id=1, source_target_pairs={{0,1},{1,2},{2,3},{3,4},{4,5},{5,6},{6,7},{7,8},{8,9},{9,10},{10,1... | collective-permute-start | bytes 737288 | tf_op jit(solution)/shard_map/ppermute | solution.py:18
  27.2 1.3 collective-permute-start.3
  28.5 1.7 %collective-permute-done.2 = f32[2,6,20,2,128]{4,3,2,1,0:T(2,128)S(1)} collective-permute-done((f32[2,6,20,2,128]{4,3,2,1,0:T(2,128)S(1)}, f32[2,6,20,2,128]{4,3,2,1,0:T(2,128)S(1)}, u32[]{:S(2)}, u32[]{:S(2)}) %collective-permute-start.2) | collective-permute-done | bytes 245792 | tf_op jit(solution)/shard_map/ppermute | solution.py:18
  30.3 3.8 %collective-permute-done.3 = f32[2,6,20,2,128]{4,3,2,1,0:T(2,128)S(1)} collective-permute-done((f32[2,6,20,2,128]{4,3,2,1,0:T(2,128)S(1)}, f32[2,6,20,2,128]{4,3,2,1,0:T(2,128)S(1)}, u32[]{:S(2)}, u32[]{:S(2)}) %collective-permute-start.3) | collective-permute-done | bytes 245792 | tf_op jit(solution)/shard_map/ppermute | solution.py:19
  34.1 0.4 pad_maximum_fusion
  34.8 0.5 fusion.4
  35.2 0.5 fusion.2
  35.7 0.5 fusion.3
  36.4 3.2 %collective-permute-start.4 = (f32[2,3,2,16,128]{4,3,2,0,1:T(8,128)S(1)}, f32[2,3,2,16,128]{4,3,2,0,1:T(8,128)S(1)}, u32[]{:S(2)}, u32[]{:S(2)}) collective-permute-start(f32[2,3,2,16,128]{4,3,2,0,1:T(8,128)S(1)} %get-tuple-element.40), channel_id=1, source_target_pairs={{0,32},{32,64},{64,96},{96,128},{128,160},{160,192},{192,224},{1,3... | collective-permute-start | bytes 294920 | tf_op jit(solution)/shard_map/ppermute | solution.py:18
  39.6 1.3 collective-permute-start.5
  41.0 0.3 collective-permute-done.4
  41.2 15.9 %collective-permute-done.5 = f32[2,3,2,16,128]{4,3,2,0,1:T(8,128)S(1)} collective-permute-done((f32[2,3,2,16,128]{4,3,2,0,1:T(8,128)S(1)}, f32[2,3,2,16,128]{4,3,2,0,1:T(8,128)S(1)}, u32[]{:S(2)}, u32[]{:S(2)}) %collective-permute-start.5) | collective-permute-done | bytes 98336 | tf_op jit(solution)/shard_map/ppermute | solution.py:19
  57.3 3.1 %collective-permute-start.6 = (f32[2,3,20,2,128]{4,3,2,0,1:T(2,128)S(1)}, f32[2,3,20,2,128]{4,3,2,0,1:T(2,128)S(1)}, u32[]{:S(2)}, u32[]{:S(2)}) collective-permute-start(f32[2,3,20,2,128]{4,3,2,0,1:T(2,128)S(1)} %get-tuple-element.38), channel_id=1, source_target_pairs={{0,1},{1,2},{2,3},{3,4},{4,5},{5,6},{6,7},{7,8},{8,9},{9,10},{10,1... | collective-permute-start | bytes 368648 | tf_op jit(solution)/shard_map/ppermute | solution.py:18
  60.4 1.3 collective-permute-start.7
  61.7 0.5 collective-permute-done.6
  62.2 3.8 %collective-permute-done.7 = f32[2,3,20,2,128]{4,3,2,0,1:T(2,128)S(1)} collective-permute-done((f32[2,3,20,2,128]{4,3,2,0,1:T(2,128)S(1)}, f32[2,3,20,2,128]{4,3,2,0,1:T(2,128)S(1)}, u32[]{:S(2)}, u32[]{:S(2)}) %collective-permute-start.7) | collective-permute-done | bytes 122912 | tf_op jit(solution)/shard_map/ppermute | solution.py:19
  66.0 0.2 pad_maximum_fusion.2
  66.5 0.4 bitcast_dynamic-update-slice_fusion
  66.9 0.4 copy-done.1
  67.8 0.4 constant_dynamic-update-slice_fusion.1
  68.2 0.4 constant_dynamic-update-slice_fusion
  68.9 0.8 maximum_bitcast_fusion
  69.9 1.6 %slice_bitcast_fusion = (f32[1,9,16,16,128]{4,3,2,1,0:T(8,128)}, f32[1,9,16,16,128]{4,3,2,1,0:T(8,128)}) fusion(f32[2,9,16,16,128]{4,3,2,0,1:T(8,128)S(1)} %pad_maximum_fusion.1), kind=kLoop, calls=%fused_computation.4 | loop fusion | bytes 4718592
  71.4 75.1 %all-reduce.2.cloned.1.call-done = f32[3,16,16,128]{3,2,1,0:T(8,128)} async-done(((f32[3,16,16,128]{3,2,1,0:T(8,128)}), f32[3,16,16,128]{3,2,1,0:T(8,128)}) %all-reduce.2.cloned.1.call-update) | async-done | bytes 393232 | tf_op jit(solution)/shard_map/psum | solution.py:205
  146.5 1.8 %copy.46 = f32[3,16,16,128]{3,2,1,0:T(8,128)} copy(f32[3,16,16,128]{3,2,1,0:T(8,128)} %all-reduce.2.cloned.1.call-done) | data formatting | bytes 786432
  (37 shorter events, 2.5 us)
Async XLA Ops:
  7.2 139.3 %all-reduce.2.cloned.1.call-start = ((), (), s32[]{:S(2)}) async-start(), calls=%async_computation | async-start | bytes 786432 | tf_op jit(solution)/shard_map/psum | solution.py:205
  12.5 6.6 %collective-permute-start = (f32[2,6,2,16,128]{4,3,2,1,0:T(8,128)S(1)}, f32[2,6,2,16,128]{4,3,2,1,0:T(8,128)S(1)}, u32[]{:S(2)}, u32[]{:S(2)}) collective-permute-start(f32[2,6,2,16,128]{4,3,2,1,0:T(8,128)S(1)} %get-tuple-element.25), channel_id=1, source_target_pairs={{0,32},{32,64},{64,96},{96,128},{128,160},{160,192},{192,224},{1,3... | collective-permute-start | bytes 589832 | tf_op jit(solution)/shard_map/ppermute | solution.py:18
  16.5 6.4 %collective-permute-start.1 = (f32[2,6,2,16,128]{4,3,2,1,0:T(8,128)S(1)}, f32[2,6,2,16,128]{4,3,2,1,0:T(8,128)S(1)}, u32[]{:S(2)}, u32[]{:S(2)}) collective-permute-start(f32[2,6,2,16,128]{4,3,2,1,0:T(8,128)S(1)} %get-tuple-element.26), channel_id=1, source_target_pairs={{32,0},{64,32},{96,64},{128,96},{160,128},{192,160},{224,192},{33,... | collective-permute-start | bytes 589832 | tf_op jit(solution)/shard_map/ppermute | solution.py:19
  18.1 10.4 %copy-start.2 = (f32[16,16,128]{2,1,0:T(8,128)S(1)}, f32[16,16,128]{2,1,0:T(8,128)}, u32[]{:S(2)}) copy-start(f32[16,16,128]{2,1,0:T(8,128)} %param.13) | copy-start | bytes 393220
  18.1 10.4 %copy-start = (f32[16,16,128]{2,1,0:T(8,128)S(1)}, f32[16,16,128]{2,1,0:T(8,128)}, u32[]{:S(2)}) copy-start(f32[16,16,128]{2,1,0:T(8,128)} %param.12) | copy-start | bytes 393220
  23.1 7.2 %collective-permute-start.2 = (f32[2,6,20,2,128]{4,3,2,1,0:T(2,128)S(1)}, f32[2,6,20,2,128]{4,3,2,1,0:T(2,128)S(1)}, u32[]{:S(2)}, u32[]{:S(2)}) collective-permute-start(f32[2,6,20,2,128]{4,3,2,1,0:T(2,128)S(1)} %get-tuple-element.27), channel_id=1, source_target_pairs={{0,1},{1,2},{2,3},{3,4},{4,5},{5,6},{6,7},{7,8},{8,9},{9,10},{10,1... | collective-permute-start | bytes 737288 | tf_op jit(solution)/shard_map/ppermute | solution.py:18
  27.2 6.9 %collective-permute-start.3 = (f32[2,6,20,2,128]{4,3,2,1,0:T(2,128)S(1)}, f32[2,6,20,2,128]{4,3,2,1,0:T(2,128)S(1)}, u32[]{:S(2)}, u32[]{:S(2)}) collective-permute-start(f32[2,6,20,2,128]{4,3,2,1,0:T(2,128)S(1)} %get-tuple-element.28), channel_id=1, source_target_pairs={{1,0},{2,1},{3,2},{4,3},{5,4},{6,5},{7,6},{8,7},{9,8},{10,9},{11,1... | collective-permute-start | bytes 737288 | tf_op jit(solution)/shard_map/ppermute | solution.py:19
  36.4 4.8 %collective-permute-start.4 = (f32[2,3,2,16,128]{4,3,2,0,1:T(8,128)S(1)}, f32[2,3,2,16,128]{4,3,2,0,1:T(8,128)S(1)}, u32[]{:S(2)}, u32[]{:S(2)}) collective-permute-start(f32[2,3,2,16,128]{4,3,2,0,1:T(8,128)S(1)} %get-tuple-element.40), channel_id=1, source_target_pairs={{0,32},{32,64},{64,96},{96,128},{128,160},{160,192},{192,224},{1,3... | collective-permute-start | bytes 294920 | tf_op jit(solution)/shard_map/ppermute | solution.py:18
  39.6 17.5 %collective-permute-start.5 = (f32[2,3,2,16,128]{4,3,2,0,1:T(8,128)S(1)}, f32[2,3,2,16,128]{4,3,2,0,1:T(8,128)S(1)}, u32[]{:S(2)}, u32[]{:S(2)}) collective-permute-start(f32[2,3,2,16,128]{4,3,2,0,1:T(8,128)S(1)} %get-tuple-element.41), channel_id=1, source_target_pairs={{32,0},{64,32},{96,64},{128,96},{160,128},{192,160},{224,192},{33,... | collective-permute-start | bytes 294920 | tf_op jit(solution)/shard_map/ppermute | solution.py:19
  57.3 5.0 %collective-permute-start.6 = (f32[2,3,20,2,128]{4,3,2,0,1:T(2,128)S(1)}, f32[2,3,20,2,128]{4,3,2,0,1:T(2,128)S(1)}, u32[]{:S(2)}, u32[]{:S(2)}) collective-permute-start(f32[2,3,20,2,128]{4,3,2,0,1:T(2,128)S(1)} %get-tuple-element.38), channel_id=1, source_target_pairs={{0,1},{1,2},{2,3},{3,4},{4,5},{5,6},{6,7},{7,8},{8,9},{9,10},{10,1... | collective-permute-start | bytes 368648 | tf_op jit(solution)/shard_map/ppermute | solution.py:18
  60.4 5.6 %collective-permute-start.7 = (f32[2,3,20,2,128]{4,3,2,0,1:T(2,128)S(1)}, f32[2,3,20,2,128]{4,3,2,0,1:T(2,128)S(1)}, u32[]{:S(2)}, u32[]{:S(2)}) collective-permute-start(f32[2,3,20,2,128]{4,3,2,0,1:T(2,128)S(1)} %get-tuple-element.39), channel_id=1, source_target_pairs={{1,0},{2,1},{3,2},{4,3},{5,4},{6,5},{7,6},{8,7},{9,8},{10,9},{11,1... | collective-permute-start | bytes 368648 | tf_op jit(solution)/shard_map/ppermute | solution.py:19
  66.4 0.9 copy-start.1
Sparse Core Ops, SparseCore 0:
  69.8 76.6 all-reduce.1
where the time goes:
time: 156 us; the launch traced here: 155 us
  waiting for transfers between devices  106 us (68%)
  starting transfers between devices  19.6 us (13%)
  between operations  15.8 us (10%)
  other arithmetic  5.89 us (4%)
  local copies, waits for them, and re-layouts  4.22 us (3%)
  matrix products  3.63 us (2%)
    psum x1, waiting for transfers between devices, body(): gradient = lax.psum(local_terms, 'shot')  75.1 us
    ppermute x4, waiting for transfers between devices, extended(): after = lax.ppermute(initial, axis, down)  27.4 us
    ppermute x4, starting transfers between devices, extended(): before = lax.ppermute(last, axis, up)  14.4 us
    ppermute x4, starting transfers between devices, extended(): after = lax.ppermute(initial, axis, down)  5.17 us
    unnamed x8, local copies, waits for them, and re-layouts  3.73 us
    ppermute x4, waiting for transfers between devices, extended(): before = lax.ppermute(last, axis, up)  3.5 us
  transfers between devices with their start and end apart: 9, of which 9 were waited for; matrix products, arithmetic and copies ran while one was open for 1% of the time, Pallas kernels for 0%

commit v1 on v0

--- a/solution.py
+++ b/solution.py
@@ -202,7 +202,7 @@
         ),
         axis=0,
     )
-    gradient = lax.psum(local_terms, "shot")
+    gradient = jnp.sum(lax.all_gather(local_terms, "shot"), axis=0)
     stepped = jnp.concatenate([velocity, stress], axis=1)
     return (stepped[:shot_count], stepped[shot_count:], gradient)
 

time: 156 us -> 112 us (0.72)
  the two profiles are of different devices: /device:TPU:1 before, /device:TPU:31 now
where the time goes in v1:
time: 112 us
  starting transfers between devices  45.7 us (41%)
  waiting for transfers between devices  42.3 us (38%)
  blocking collectives  9.13 us (8%)
  other arithmetic  5.97 us (5%)
  matrix products  3.63 us (3%)
  local copies, waits for them, and re-layouts  2.47 us (2%)
  between operations  2.41 us (2%)
    ppermute x4, waiting for transfers between devices, extended(): after = lax.ppermute(initial, axis, down)  39.2 us
    ppermute x4, starting transfers between devices, extended(): before = lax.ppermute(last, axis, up)  36.5 us
    all_gather x1, blocking collectives, body(): gradient = jnp.sum(lax.all_gather(local_terms, 'shot'), axis=0)  9.13 us
    ppermute x4, starting transfers between devices, extended(): after = lax.ppermute(initial, axis, down)  9.12 us
    ppermute x4, waiting for transfers between devices, extended(): before = lax.ppermute(last, axis, up)  3.08 us
    dot_general x6, matrix products, derive(): jnp.einsum('...k,ki->...i', core, depth_table(core.shape[-1], upward), pr...  2.58 us
  transfers between devices with their start and end apart: 8, of which 7 were waited for; matrix products, arithmetic and copies ran while one was open for 0% of the time, Pallas kernels for 0%

profile of v1, /device:TPU:31, one launch (start us, length us, event | category | flops | bytes accessed | tf_op | source)
XLA Modules:
  0.0 111.6 jit_solution(1189264514498616408)
XLA Ops:
  2.1 0.7 and_select_fusion
  3.0 1.1 fusion.53
  4.0 1.8 %fusion.168 = (f32[1,3,16,16,128]{4,3,2,1,0:T(8,128)S(1)}, f32[1,3,16,16,128]{4,3,2,1,0:T(8,128)S(1)}, f32[1,3,16,16,128]{4,3,2,1,0:T(8,128)S(1)}, f32[1,3,16,16...) fusion(f32[1,9,16,16,128]{4,3,2,1,0:T(8,128)} %param.9, ...), kind=kLoop, calls=%fused_computation.264 | loop fusion | flops 196608 | bytes 4980736 | tf_op jit(solution)/shard_map/vmap()/slice | solution.py:165
  5.9 15.1 %collective-permute-start = (f32[2,6,2,16,128]{4,3,2,1,0:T(8,128)S(1)}, f32[2,6,2,16,128]{4,3,2,1,0:T(8,128)S(1)}, u32[]{:S(2)}, u32[]{:S(2)}) collective-permute-start(f32[2,6,2,16,128]{4,3,2,1,0:T(8,128)S(1)} %get-tuple-element.28), channel_id=1, source_target_pairs={{0,32},{32,64},{64,96},{96,128},{128,160},{160,192},{192,224},{1,3... | collective-permute-start | bytes 589832 | tf_op jit(solution)/shard_map/ppermute | solution.py:18
  21.0 1.9 %collective-permute-start.1 = (f32[2,6,2,16,128]{4,3,2,1,0:T(8,128)S(1)}, f32[2,6,2,16,128]{4,3,2,1,0:T(8,128)S(1)}, u32[]{:S(2)}, u32[]{:S(2)}) collective-permute-start(f32[2,6,2,16,128]{4,3,2,1,0:T(8,128)S(1)} %get-tuple-element.29), channel_id=1, source_target_pairs={{32,0},{64,32},{96,64},{128,96},{160,128},{192,160},{224,192},{33,... | collective-permute-start | bytes 589832 | tf_op jit(solution)/shard_map/ppermute | solution.py:19
  23.2 1.3 %collective-permute-done = f32[2,6,2,16,128]{4,3,2,1,0:T(8,128)S(1)} collective-permute-done((f32[2,6,2,16,128]{4,3,2,1,0:T(8,128)S(1)}, f32[2,6,2,16,128]{4,3,2,1,0:T(8,128)S(1)}, u32[]{:S(2)}, u32[]{:S(2)}) %collective-permute-start) | collective-permute-done | bytes 196640 | tf_op jit(solution)/shard_map/ppermute | solution.py:18
  24.5 14.6 %collective-permute-done.1 = f32[2,6,2,16,128]{4,3,2,1,0:T(8,128)S(1)} collective-permute-done((f32[2,6,2,16,128]{4,3,2,1,0:T(8,128)S(1)}, f32[2,6,2,16,128]{4,3,2,1,0:T(8,128)S(1)}, u32[]{:S(2)}, u32[]{:S(2)}) %collective-permute-start.1) | collective-permute-done | bytes 196640 | tf_op jit(solution)/shard_map/ppermute | solution.py:19
  39.3 15.6 %collective-permute-start.2 = (f32[2,6,20,2,128]{4,3,2,1,0:T(2,128)S(1)}, f32[2,6,20,2,128]{4,3,2,1,0:T(2,128)S(1)}, u32[]{:S(2)}, u32[]{:S(2)}) collective-permute-start(f32[2,6,20,2,128]{4,3,2,1,0:T(2,128)S(1)} %get-tuple-element.30), channel_id=1, source_target_pairs={{0,1},{1,2},{2,3},{3,4},{4,5},{5,6},{6,7},{7,8},{8,9},{9,10},{10,1... | collective-permute-start | bytes 737288 | tf_op jit(solution)/shard_map/ppermute | solution.py:18
  54.9 1.9 %collective-permute-start.3 = (f32[2,6,20,2,128]{4,3,2,1,0:T(2,128)S(1)}, f32[2,6,20,2,128]{4,3,2,1,0:T(2,128)S(1)}, u32[]{:S(2)}, u32[]{:S(2)}) collective-permute-start(f32[2,6,20,2,128]{4,3,2,1,0:T(2,128)S(1)} %get-tuple-element.31), channel_id=1, source_target_pairs={{1,0},{2,1},{3,2},{4,3},{5,4},{6,5},{7,6},{8,7},{9,8},{10,9},{11,1... | collective-permute-start | bytes 737288 | tf_op jit(solution)/shard_map/ppermute | solution.py:19
  57.0 1.7 %collective-permute-done.2 = f32[2,6,20,2,128]{4,3,2,1,0:T(2,128)S(1)} collective-permute-done((f32[2,6,20,2,128]{4,3,2,1,0:T(2,128)S(1)}, f32[2,6,20,2,128]{4,3,2,1,0:T(2,128)S(1)}, u32[]{:S(2)}, u32[]{:S(2)}) %collective-permute-start.2) | collective-permute-done | bytes 245792 | tf_op jit(solution)/shard_map/ppermute | solution.py:18
  58.7 5.9 %collective-permute-done.3 = f32[2,6,20,2,128]{4,3,2,1,0:T(2,128)S(1)} collective-permute-done((f32[2,6,20,2,128]{4,3,2,1,0:T(2,128)S(1)}, f32[2,6,20,2,128]{4,3,2,1,0:T(2,128)S(1)}, u32[]{:S(2)}, u32[]{:S(2)}) %collective-permute-start.3) | collective-permute-done | bytes 245792 | tf_op jit(solution)/shard_map/ppermute | solution.py:19
  64.6 0.4 pad_maximum_fusion
  65.0 0.2 slice_bitcast_fusion.10
  65.3 0.5 fusion.4
  65.7 0.5 fusion.2
  66.2 0.5 fusion.3
  66.9 1.9 %collective-permute-start.4 = (f32[2,3,2,16,128]{4,3,2,0,1:T(8,128)S(1)}, f32[2,3,2,16,128]{4,3,2,0,1:T(8,128)S(1)}, u32[]{:S(2)}, u32[]{:S(2)}) collective-permute-start(f32[2,3,2,16,128]{4,3,2,0,1:T(8,128)S(1)} %get-tuple-element.43), channel_id=1, source_target_pairs={{0,32},{32,64},{64,96},{96,128},{128,160},{160,192},{192,224},{1,3... | collective-permute-start | bytes 294920 | tf_op jit(solution)/shard_map/ppermute | solution.py:18
  68.9 3.4 %collective-permute-start.5 = (f32[2,3,2,16,128]{4,3,2,0,1:T(8,128)S(1)}, f32[2,3,2,16,128]{4,3,2,0,1:T(8,128)S(1)}, u32[]{:S(2)}, u32[]{:S(2)}) collective-permute-start(f32[2,3,2,16,128]{4,3,2,0,1:T(8,128)S(1)} %get-tuple-element.44), channel_id=1, source_target_pairs={{32,0},{64,32},{96,64},{128,96},{160,128},{192,160},{224,192},{33,... | collective-permute-start | bytes 294920 | tf_op jit(solution)/shard_map/ppermute | solution.py:19
  72.3 12.9 %collective-permute-done.5 = f32[2,3,2,16,128]{4,3,2,0,1:T(8,128)S(1)} collective-permute-done((f32[2,3,2,16,128]{4,3,2,0,1:T(8,128)S(1)}, f32[2,3,2,16,128]{4,3,2,0,1:T(8,128)S(1)}, u32[]{:S(2)}, u32[]{:S(2)}) %collective-permute-start.5) | collective-permute-done | bytes 98336 | tf_op jit(solution)/shard_map/ppermute | solution.py:19
  85.3 3.9 %collective-permute-start.6 = (f32[2,3,20,2,128]{4,3,2,0,1:T(2,128)S(1)}, f32[2,3,20,2,128]{4,3,2,0,1:T(2,128)S(1)}, u32[]{:S(2)}, u32[]{:S(2)}) collective-permute-start(f32[2,3,20,2,128]{4,3,2,0,1:T(2,128)S(1)} %get-tuple-element.41), channel_id=1, source_target_pairs={{0,1},{1,2},{2,3},{3,4},{4,5},{5,6},{6,7},{7,8},{8,9},{9,10},{10,1... | collective-permute-start | bytes 368648 | tf_op jit(solution)/shard_map/ppermute | solution.py:18
  89.2 1.9 %collective-permute-start.7 = (f32[2,3,20,2,128]{4,3,2,0,1:T(2,128)S(1)}, f32[2,3,20,2,128]{4,3,2,0,1:T(2,128)S(1)}, u32[]{:S(2)}, u32[]{:S(2)}) collective-permute-start(f32[2,3,20,2,128]{4,3,2,0,1:T(2,128)S(1)} %get-tuple-element.42), channel_id=1, source_target_pairs={{1,0},{2,1},{3,2},{4,3},{5,4},{6,5},{7,6},{8,7},{9,8},{10,9},{11,1... | collective-permute-start | bytes 368648 | tf_op jit(solution)/shard_map/ppermute | solution.py:19
  91.2 5.7 %collective-permute-done.7 = f32[2,3,20,2,128]{4,3,2,0,1:T(2,128)S(1)} collective-permute-done((f32[2,3,20,2,128]{4,3,2,0,1:T(2,128)S(1)}, f32[2,3,20,2,128]{4,3,2,0,1:T(2,128)S(1)}, u32[]{:S(2)}, u32[]{:S(2)}) %collective-permute-start.7) | collective-permute-done | bytes 122912 | tf_op jit(solution)/shard_map/ppermute | solution.py:19
  96.9 0.2 pad_maximum_fusion.2
  97.5 0.4 bitcast_dynamic-update-slice_fusion
  97.9 0.4 copy-done.1
  98.3 0.2 slice_add_fusion
  98.8 0.4 constant_dynamic-update-slice_fusion.1
  99.2 0.4 constant_dynamic-update-slice_fusion
  99.7 0.2 pad_maximum_fusion.1
  100.1 1.6 %slice_bitcast_fusion = (f32[1,9,16,16,128]{4,3,2,1,0:T(8,128)}, f32[1,9,16,16,128]{4,3,2,1,0:T(8,128)}) fusion(f32[2,9,16,16,128]{4,3,2,0,1:T(8,128)S(1)} %pad_maximum_fusion.1), kind=kLoop, calls=%fused_computation.4 | loop fusion | bytes 4718592
  101.6 9.1 %all_gather.4 = f32[2,3,16,16,128]{4,3,2,1,0:T(8,128)S(1)} all-gather(f32[1,3,16,16,128]{4,3,2,1,0:T(8,128)S(1)} %pad_maximum_fusion.4), channel_id=1, replica_groups=mesh['shot'=2,'tx'=8,'ty'=32] {'shot'}, dimensions={0}, use_global_device_ids=true | all-gather | bytes 1179648 | tf_op jit(solution)/shard_map/all_gather | solution.py:205
  110.8 0.8 reduce_sum.33
  (35 shorter events, 2.0 us)
Async XLA Ops:
  5.9 18.7 %collective-permute-start = (f32[2,6,2,16,128]{4,3,2,1,0:T(8,128)S(1)}, f32[2,6,2,16,128]{4,3,2,1,0:T(8,128)S(1)}, u32[]{:S(2)}, u32[]{:S(2)}) collective-permute-start(f32[2,6,2,16,128]{4,3,2,1,0:T(8,128)S(1)} %get-tuple-element.28), channel_id=1, source_target_pairs={{0,32},{32,64},{64,96},{96,128},{128,160},{160,192},{192,224},{1,3... | collective-permute-start | bytes 589832 | tf_op jit(solution)/shard_map/ppermute | solution.py:18
  21.0 18.2 %collective-permute-start.1 = (f32[2,6,2,16,128]{4,3,2,1,0:T(8,128)S(1)}, f32[2,6,2,16,128]{4,3,2,1,0:T(8,128)S(1)}, u32[]{:S(2)}, u32[]{:S(2)}) collective-permute-start(f32[2,6,2,16,128]{4,3,2,1,0:T(8,128)S(1)} %get-tuple-element.29), channel_id=1, source_target_pairs={{32,0},{64,32},{96,64},{128,96},{160,128},{192,160},{224,192},{33,... | collective-permute-start | bytes 589832 | tf_op jit(solution)/shard_map/ppermute | solution.py:19
  23.2 33.7 %copy-start.2 = (f32[16,16,128]{2,1,0:T(8,128)S(1)}, f32[16,16,128]{2,1,0:T(8,128)}, u32[]{:S(2)}) copy-start(f32[16,16,128]{2,1,0:T(8,128)} %param.13) | copy-start | bytes 393220
  23.2 33.7 %copy-start = (f32[16,16,128]{2,1,0:T(8,128)S(1)}, f32[16,16,128]{2,1,0:T(8,128)}, u32[]{:S(2)}) copy-start(f32[16,16,128]{2,1,0:T(8,128)} %param.12) | copy-start | bytes 393220
  39.3 19.3 %collective-permute-start.2 = (f32[2,6,20,2,128]{4,3,2,1,0:T(2,128)S(1)}, f32[2,6,20,2,128]{4,3,2,1,0:T(2,128)S(1)}, u32[]{:S(2)}, u32[]{:S(2)}) collective-permute-start(f32[2,6,20,2,128]{4,3,2,1,0:T(2,128)S(1)} %get-tuple-element.30), channel_id=1, source_target_pairs={{0,1},{1,2},{2,3},{3,4},{4,5},{5,6},{6,7},{7,8},{8,9},{9,10},{10,1... | collective-permute-start | bytes 737288 | tf_op jit(solution)/shard_map/ppermute | solution.py:18
  54.9 9.7 %collective-permute-start.3 = (f32[2,6,20,2,128]{4,3,2,1,0:T(2,128)S(1)}, f32[2,6,20,2,128]{4,3,2,1,0:T(2,128)S(1)}, u32[]{:S(2)}, u32[]{:S(2)}) collective-permute-start(f32[2,6,20,2,128]{4,3,2,1,0:T(2,128)S(1)} %get-tuple-element.31), channel_id=1, source_target_pairs={{1,0},{2,1},{3,2},{4,3},{5,4},{6,5},{7,6},{8,7},{9,8},{10,9},{11,1... | collective-permute-start | bytes 737288 | tf_op jit(solution)/shard_map/ppermute | solution.py:19
  66.9 5.4 %collective-permute-start.4 = (f32[2,3,2,16,128]{4,3,2,0,1:T(8,128)S(1)}, f32[2,3,2,16,128]{4,3,2,0,1:T(8,128)S(1)}, u32[]{:S(2)}, u32[]{:S(2)}) collective-permute-start(f32[2,3,2,16,128]{4,3,2,0,1:T(8,128)S(1)} %get-tuple-element.43), channel_id=1, source_target_pairs={{0,32},{32,64},{64,96},{96,128},{128,160},{160,192},{192,224},{1,3... | collective-permute-start | bytes 294920 | tf_op jit(solution)/shard_map/ppermute | solution.py:18
  68.9 16.4 %collective-permute-start.5 = (f32[2,3,2,16,128]{4,3,2,0,1:T(8,128)S(1)}, f32[2,3,2,16,128]{4,3,2,0,1:T(8,128)S(1)}, u32[]{:S(2)}, u32[]{:S(2)}) collective-permute-start(f32[2,3,2,16,128]{4,3,2,0,1:T(8,128)S(1)} %get-tuple-element.44), channel_id=1, source_target_pairs={{32,0},{64,32},{96,64},{128,96},{160,128},{192,160},{224,192},{33,... | collective-permute-start | bytes 294920 | tf_op jit(solution)/shard_map/ppermute | solution.py:19
  85.3 5.9 %collective-permute-start.6 = (f32[2,3,20,2,128]{4,3,2,0,1:T(2,128)S(1)}, f32[2,3,20,2,128]{4,3,2,0,1:T(2,128)S(1)}, u32[]{:S(2)}, u32[]{:S(2)}) collective-permute-start(f32[2,3,20,2,128]{4,3,2,0,1:T(2,128)S(1)} %get-tuple-element.41), channel_id=1, source_target_pairs={{0,1},{1,2},{2,3},{3,4},{4,5},{5,6},{6,7},{7,8},{8,9},{9,10},{10,1... | collective-permute-start | bytes 368648 | tf_op jit(solution)/shard_map/ppermute | solution.py:18
  89.2 7.7 %collective-permute-start.7 = (f32[2,3,20,2,128]{4,3,2,0,1:T(2,128)S(1)}, f32[2,3,20,2,128]{4,3,2,0,1:T(2,128)S(1)}, u32[]{:S(2)}, u32[]{:S(2)}) collective-permute-start(f32[2,3,20,2,128]{4,3,2,0,1:T(2,128)S(1)} %get-tuple-element.42), channel_id=1, source_target_pairs={{1,0},{2,1},{3,2},{4,3},{5,4},{6,5},{7,6},{8,7},{9,8},{10,9},{11,1... | collective-permute-start | bytes 368648 | tf_op jit(solution)/shard_map/ppermute | solution.py:19
  97.4 0.9 copy-start.1
